TPU v7x, 512 devices: a whole 4x4x16 slice. The times are simulated.
512 devices in a mesh: dp: 16 (over x_hi, y, core), ctx: 32 (over x_lo, z).
Axes of the slice: x: 4 (x_hi: 2, x_lo: 2; x = x_hi * 2 + x_lo), y: 4, z: 16, core: 2. Of those that a mesh axis runs over, the one named last changes fastest.
Arguments:
- query: bfloat16 [16, 4096, 512], P('dp', 'ctx'), may hold values from -6 to 6
- key: bfloat16 [16, 4096, 512], P('dp', 'ctx'), may hold values from -6 to 6
- value: bfloat16 [16, 4096, 512], P('dp', 'ctx'), may hold values from -6 to 6
- out_grad: bfloat16 [16, 4096, 1024], P('dp', 'ctx'), may hold values from -6 to 6
- w_out: bfloat16 [512, 1024], P('dp'), may hold values from -0.25 to 0.25
- band_tiles: int32 [32, 3], replicated, may hold values from 0 to 1, as said below
- global_blocks: int32 [3], replicated, may hold values from 0 to 31, as said below
Outputs:
- query_grad: bfloat16 [16, 4096, 512], P('dp', 'ctx')
- key_grad: bfloat16 [16, 4096, 512], P('dp', 'ctx')
- value_grad: bfloat16 [16, 4096, 512], P('dp', 'ctx')
- w_out_grad: float32 [512, 1024], P(('dp', 'ctx'))
Inputs may be any that keep to these rules, and one draw needn't show every extreme that they name: band_tiles[a, c] = 1 lists the tile of query block a and key block a + c - 1; column 1 is 1 in every row; entries that point outside the utterance are ignored. `global_blocks`: distinct block numbers; 0 and 31 are among them.
All inputs are finite; a program needn't handle non-finite values.
Results may differ from a plain program's by a relative error of at most 0.03.
Values may be sent and summed in bfloat16 or wider, within the bound.
No kernel may reach another device: no remote copies, remote signals or barrier semaphores. Data moves between devices by JAX's collectives and lax.ppermute only.
A program may use at most 64 MiB of HBM per device.

v0:
```python
import jax
import jax.numpy as jnp
from jax import lax
from jax.sharding import PartitionSpec as P

HEADS = 4
HDIM = 128
BLK = 128


def padded(shard, sides, width):
    for axis, dim in sides:
        size, length = (lax.axis_size(axis), shard.shape[dim])
        up = [(i, (i + 1) % size) for i in range(size - 1)]
        down = [(j, i) for i, j in up]
        last = lax.slice_in_dim(shard, length - width, length, axis=dim)
        leading = lax.slice_in_dim(shard, 0, width, axis=dim)
        before = lax.ppermute(last, axis, up)
        after = lax.ppermute(leading, axis, down)
        shard = jnp.concatenate([before, shard, after], axis=dim)
    return shard


def from_behind(shard, axis, by):
    size = lax.axis_size(axis)
    pairs = [(i, i + by) for i in range(size) if 0 <= i + by < size]
    return lax.ppermute(shard, axis, pairs)


def tile_mask(band_tiles, global_blocks, q_first, q_count, k_first, k_count, n_blocks, band, blk):
    q_ids = q_first + jnp.arange(q_count, dtype=jnp.int32)
    k_ids = k_first + jnp.arange(k_count, dtype=jnp.int32)
    offset = k_ids[None, :] - q_ids[:, None]
    inside = (jnp.abs(offset) <= band) & (k_ids[None, :] >= 0) & (k_ids[None, :] < n_blocks)
    inside = inside & (q_ids[:, None] >= 0) & (q_ids[:, None] < n_blocks)
    table_hit = (q_ids[:, None] == jnp.arange(n_blocks, dtype=jnp.int32)[None, :]).astype(jnp.int32)
    rows_of = jnp.dot(table_hit, band_tiles)
    column = offset + band
    slots = jnp.arange(2 * band + 1, dtype=jnp.int32)
    chosen = jnp.sum(
        rows_of[:, None, :] * (column[:, :, None] == slots[None, None, :]).astype(jnp.int32), axis=2
    )
    shared = jnp.any(k_ids[:, None] == global_blocks[None, :], axis=1)
    tile = inside & (chosen > 0) & jnp.logical_not(shared)[None, :]
    full = jnp.broadcast_to(tile[:, None, :, None], (q_count, blk, k_count, blk))
    return full.reshape(q_count * blk, k_count * blk)


def contract_rows(left, right):
    return lax.dot_general(
        left, right, (((0,), (0,)), ((), ())), preferred_element_type=jnp.float32
    )


def contract_cols(left, right):
    return lax.dot_general(
        left, right, (((1,), (1,)), ((), ())), preferred_element_type=jnp.float32
    )


def on_device(query, key, value, out_grad, w_out, band_tiles, global_blocks):
    q_own = query[0]
    k_own = key[0]
    v_own = value[0]
    grad_own = out_grad[0]
    rows, width = q_own.shape
    per_dev = rows // BLK
    n_blocks = per_dev * lax.axis_size("ctx")
    first = lax.axis_index("ctx") * per_dev
    scale = HDIM ** (-0.5)
    d_out = contract_cols(grad_own, lax.all_gather(w_out, "dp", axis=0, tiled=True)).astype(
        jnp.bfloat16
    )
    pair = jnp.stack([k_own, v_own])
    wide = padded(pair, (("ctx", 1),), rows)
    local_ids = first + jnp.arange(per_dev, dtype=jnp.int32)
    pick = global_blocks[:, None] == local_ids[None, :]
    owned = jnp.einsum(
        "gb,cbrh->cgrh",
        pick.astype(jnp.bfloat16),
        pair.reshape(2, per_dev, BLK, width),
        preferred_element_type=jnp.float32,
    )
    shared = lax.psum(owned.astype(jnp.bfloat16), "ctx").reshape(2, -1, width)
    keys = jnp.concatenate([wide[0], shared[0]], 0)
    vals = jnp.concatenate([wide[1], shared[1]], 0)
    n_glob = shared.shape[1]
    band = tile_mask(
        band_tiles,
        global_blocks,
        first,
        per_dev,
        first - per_dev,
        3 * per_dev,
        n_blocks,
        per_dev,
        BLK,
    )
    mask = jnp.concatenate([band, jnp.ones((rows, n_glob), bool)], 1)
    outs, grads, key_parts, value_parts, maxima, totals, deltas = ([], [], [], [], [], [], [])
    for head in range(HEADS):
        low, high = (head * HDIM, (head + 1) * HDIM)
        q_head = q_own[:, low:high]
        k_head = keys[:, low:high]
        v_head = vals[:, low:high]
        d_head = d_out[:, low:high]
        scores = jnp.where(mask, contract_cols(q_head, k_head) * scale, -jnp.inf)
        peak = jnp.max(scores, axis=1, keepdims=True)
        expo = jnp.where(mask, jnp.exp(scores - peak), 0.0)
        total = jnp.sum(expo, axis=1, keepdims=True)
        prob = expo / total
        prob_low = prob.astype(jnp.bfloat16)
        out_head = jnp.dot(prob_low, v_head, preferred_element_type=jnp.float32).astype(
            jnp.bfloat16
        )
        delta = jnp.sum(
            d_head.astype(jnp.float32) * out_head.astype(jnp.float32), axis=1, keepdims=True
        )
        slope = contract_cols(d_head, v_head)
        dscore = (prob * (slope - delta)).astype(jnp.bfloat16)
        grads.append(
            (scale * jnp.dot(dscore, k_head, preferred_element_type=jnp.float32)).astype(
                jnp.bfloat16
            )
        )
        outs.append(out_head)
        maxima.append(peak)
        totals.append(total)
        deltas.append(delta)
        key_parts.append(scale * contract_rows(dscore, q_head))
        value_parts.append(contract_rows(prob_low, d_head))
    attended = jnp.concatenate(outs, 1)
    query_grad = jnp.concatenate(grads, 1)
    key_part = jnp.concatenate(key_parts, 1)
    value_part = jnp.concatenate(value_parts, 1)
    lower = jnp.stack([key_part[:rows], value_part[:rows]])
    upper = jnp.stack([key_part[2 * rows : 3 * rows], value_part[2 * rows : 3 * rows]])
    from_upper = from_behind(lower.astype(jnp.bfloat16), "ctx", -1).astype(lower.dtype)
    from_lower = from_behind(upper.astype(jnp.bfloat16), "ctx", 1).astype(upper.dtype)
    own = (
        jnp.stack([key_part[rows : 2 * rows], value_part[rows : 2 * rows]])
        + from_upper
        + from_lower
    )
    glob_part = jnp.stack([key_part[3 * rows :], value_part[3 * rows :]])
    glob_sum = (
        lax.psum(glob_part.astype(jnp.bfloat16), "ctx")
        .astype(jnp.float32)
        .reshape(2, -1, BLK, width)
    )
    back = jnp.einsum(
        "gb,cgrh->cbrh", pick.astype(jnp.float32), glob_sum, precision=lax.Precision.HIGHEST
    ).reshape(2, rows, width)
    summed = (own + back).astype(jnp.bfloat16)
    w_grad = lax.psum_scatter(
        contract_rows(attended, grad_own), ("dp", "ctx"), scatter_dimension=0, tiled=True
    )
    return (query_grad[None], summed[0][None], summed[1][None], w_grad)


def solution(mesh):
    return jax.shard_map(
        on_device,
        mesh=mesh,
        in_specs=(
            P("dp", "ctx", None),
            P("dp", "ctx", None),
            P("dp", "ctx", None),
            P("dp", "ctx", None),
            P("dp", None),
            P(),
            P(),
        ),
        out_specs=(
            P("dp", "ctx", None),
            P("dp", "ctx", None),
            P("dp", "ctx", None),
            P(("dp", "ctx"), None),
        ),
        check_vma=False,
    )
```

profile of v0, /device:TPU:1, one launch (start us, length us, event | category | flops | bytes accessed | tf_op | source)
XLA Modules:
  0.0 1029.6 jit_solution(11150613608643000979)
XLA Ops:
  10.7 1.1 fusion.18
  11.9 1.3 collective-permute-start.1
  13.2 5.0 collective-permute-start
  18.9 1.1 collective-permute-done.1
  20.0 1.5 collective-permute-done
  21.6 231.9 %all-reduce.6.cloned.1.call-done = bf16[2,3,128,512]{3,2,1,0:T(8,128)(2,1)} async-done(((bf16[2,3,128,512]{3,2,1,0:T(8,128)(2,1)}), bf16[2,3,128,512]{3,2,1,0:T(8,128)(2,1)}) %all-reduce.6.cloned.1.call-update) | async-done | bytes 786448 | tf_op jit(solution)/shard_map/psum | solution.py:84
  253.5 1.2 fusion.97
  256.7 1.0 convolution_convert_fusion.3
  257.7 1.0 convolution_convert_fusion.2
  258.7 1.0 convolution_convert_fusion.1
  259.8 1.7 convolution_convert_fusion
  264.0 1.0 multiply_reduce_fusion.3
  272.3 2.1 pad_maximum_fusion.3
  274.6 1.6 pad_maximum_fusion.5
  276.2 3.1 collective-permute-start.3
  279.5 1.3 pad_maximum_fusion
  280.8 1.8 fusion.30
  283.6 1.3 collective-permute-start.2
  284.9 1.0 slice_bitcast_fusion.5
  285.9 239.5 %all-reduce.8.cloned.1.call-done = bf16[2,3,128,512]{3,2,1,0:T(8,128)(2,1)} async-done(((bf16[2,3,128,512]{3,2,1,0:T(8,128)(2,1)}), bf16[2,3,128,512]{3,2,1,0:T(8,128)(2,1)}) %all-reduce.8.cloned.1.call-update) | async-done | bytes 786448 | tf_op jit(solution)/shard_map/psum | solution.py:147
  525.4 1.9 fusion.16
  527.3 1.1 fusion.21
  529.1 492.0 %all-reduce.10.cloned.1.call-done = f32[512,1024]{1,0:T(8,128)} async-done(((f32[512,1024]{1,0:T(8,128)}), f32[512,1024]{1,0:T(8,128)}) %all-reduce.10.cloned.1.call-update) | async-done | bytes 2097168
  1021.1 1.4 constant_dynamic-slice_fusion
  (130 shorter events, 17.0 us)
Async XLA Ops:
  8.0 251.8 %copy-start = (bf16[1,128,1024]{2,1,0:T(8,128)(2,1)S(1)}, bf16[1,128,1024]{2,1,0:T(8,128)(2,1)}, u32[]{:S(2)}) copy-start(bf16[1,128,1024]{2,1,0:T(8,128)(2,1)} %param.10) | copy-start | bytes 786436
  8.0 245.5 %all-reduce.6.cloned.1.call-start = ((), (), s32[]{:S(2)}) async-start(), calls=%async_computation | async-start | bytes 1572864 | tf_op jit(solution)/shard_map/psum | solution.py:84
  9.0 9.3 copy-start.34
  9.0 9.4 copy-start.24
  11.8 247.9 %all-gather.2.cloned.1.call-start = ((), (), s32[]{:S(2)}) async-start(), calls=%async_computation.1 | async-start | bytes 1114112 | tf_op jit(solution)/shard_map/all_gather | solution.py:71
  11.9 8.1 collective-permute-start.1
  13.2 8.3 collective-permute-start
  18.2 507.2 %all-reduce.8.cloned.1.call-start = ((), (), s32[]{:S(2)}) async-start(), calls=%async_computation.2 | async-start | bytes 1572864 | tf_op jit(solution)/shard_map/psum | solution.py:147
  21.6 236.1 %copy-start.9 = (bf16[384,512]{1,0:T(8,128)(2,1)}, bf16[384,512]{1,0:T(8,128)(2,1)S(1)}, u32[]{:S(2)}) copy-start(bf16[384,512]{1,0:T(8,128)(2,1)S(1)} %get-tuple-element.31) | copy-start | bytes 1179652
  21.6 233.2 %copy-start.13 = (bf16[1,128,512]{2,1,0:T(8,128)(2,1)S(1)}, bf16[1,128,512]{2,1,0:T(8,128)(2,1)}, u32[]{:S(2)}) copy-start(bf16[1,128,512]{2,1,0:T(8,128)(2,1)} %param.7) | copy-start | bytes 393220
  254.7 3.1 copy-start.11
  255.3 8.1 copy-start.3
  255.6 6.9 copy-start.5
  255.9 2.8 copy-start.25
  255.9 5.6 copy-start.7
  256.7 2.0 copy-start.32
  259.7 2.7 copy-start.31
  263.9 4.5 copy-start.1
  271.6 7.7 copy-start.2
  272.3 2.2 copy-start.16
  274.5 746.6 %all-reduce.10.cloned.1.call-start = ((), (), s32[]{:S(2)}) async-start(), calls=%async_computation.3 | async-start | bytes 4194304
  276.2 251.1 %collective-permute-start.3 = (bf16[2,128,512]{2,1,0:T(8,128)(2,1)}, bf16[2,128,512]{2,1,0:T(8,128)(2,1)}, u32[]{:S(2)}, u32[]{:S(2)}) collective-permute-start(bf16[2,128,512]{2,1,0:T(8,128)(2,1)} %pad_maximum_fusion.5), channel_id=1, source_target_pairs={{0,1},{1,2},{2,3},{3,4},{4,5},{5,6},{6,7},{7,8},{8,9},{9,10},{10,1... | collective-permute-start | bytes 786440 | tf_op jit(solution)/shard_map/ppermute | solution.py:27
  282.6 242.8 %copy-start.35 = (s32[3]{0:T(128)S(1)}, s32[3]{0:T(128)}, u32[]{:S(2)}) copy-start(s32[3]{0:T(128)} %param.13) | copy-start | bytes 40
  283.6 243.7 %collective-permute-start.2 = (bf16[2,128,512]{2,1,0:T(8,128)(2,1)S(1)}, bf16[2,128,512]{2,1,0:T(8,128)(2,1)S(1)}, u32[]{:S(2)}, u32[]{:S(2)}) collective-permute-start(bf16[2,128,512]{2,1,0:T(8,128)(2,1)S(1)} %pad_maximum_fusion.4), channel_id=1, source_target_pairs={{1,0},{2,1},{3,2},{4,3},{5,4},{6,5},{7,6},{8,7},{9,8},{10,9},{11,1... | collective-permute-start | bytes 786440 | tf_op jit(solution)/shard_map/ppermute | solution.py:27
  (20 other events, 24.1 us)
Sparse Core Ops, SparseCore 0:
  11.9 241.5 all-reduce.5
  274.6 250.7 all-reduce.7
  530.7 490.3 all-reduce.9
Sparse Core Ops, SparseCore 1:
  18.3 65.6 all-gather.1
where the time goes:
time: 1030 us
  waiting for transfers between devices  966 us (94%)
  between operations  15.8 us (2%)
  matrix products  15.2 us (1%)
  local copies, waits for them, and re-layouts  12.2 us (1%)
  starting transfers between devices  10.9 us (1%)
    unnamed x5, waiting for transfers between devices  492 us
    psum x1, waiting for transfers between devices, on_device(): lax.psum(glob_part.astype(jnp.bfloat16), 'ctx').astype(jnp.float32)  240 us
    psum x1, waiting for transfers between devices, on_device(): shared = lax.psum(owned.astype(jnp.bfloat16), 'ctx').reshape(2, -1, width)  232 us
  transfers between devices with their start and end apart: 8, of which 5 were waited for; matrix products, arithmetic and copies ran while one was open for 2% of the time, Pallas kernels for 0%

commit v1 on v0

--- a/solution.py
+++ b/solution.py
@@ -6,6 +6,11 @@
 HEADS = 4
 HDIM = 128
 BLK = 128
+
+
+def add_all(x, name):
+    parts = lax.all_gather(x, name)
+    return jnp.sum(parts, axis=0)
 
 
 def padded(shard, sides, width):
@@ -81,7 +86,7 @@
         pair.reshape(2, per_dev, BLK, width),
         preferred_element_type=jnp.float32,
     )
-    shared = lax.psum(owned.astype(jnp.bfloat16), "ctx").reshape(2, -1, width)
+    shared = add_all(owned.astype(jnp.bfloat16), "ctx").reshape(2, -1, width)
     keys = jnp.concatenate([wide[0], shared[0]], 0)
     vals = jnp.concatenate([wide[1], shared[1]], 0)
     n_glob = shared.shape[1]

time: 1030 us -> 1130 us (1.097)
  waiting for transfers between devices: 966 us -> 1060 us
    all_gather x0 -> x1, waiting for transfers between devices: none -> 283 us  [add_all(): parts = lax.all_gather(x, name)]
    psum x1 -> x0, waiting for transfers between devices: 232 us -> none  [on_device(): shared = lax.psum(owned.astype(jnp.bfloat16), 'ctx').reshape(2, -1, width)]
    all_gather x1, waiting for transfers between devices: 0.01 us -> 55.8 us  [on_device(): lax.all_gather(w_out, 'dp', axis=0, tiled=True)]
    psum x1, waiting for transfers between devices: 240 us -> 225 us  [on_device(): lax.psum(glob_part.astype(jnp.bfloat16), 'ctx').astype(jnp.float32)]
    reduce_sum x0 -> x1, other arithmetic: none -> 13 us  [add_all(): return jnp.sum(parts, axis=0)]
  transfers between devices with their start and end apart: 8 -> 8, of which waited for: 5 -> 6; matrix products, arithmetic and copies ran while one was open for 2% -> 1% of each run, Pallas kernels for 0% -> 0%
where the time goes in v1:
time: 1130 us
  waiting for transfers between devices  1060 us (94%)
  other arithmetic  20.9 us (2%)
  between operations  14.2 us (1%)
  matrix products  12.6 us (1%)
    unnamed x5, waiting for transfers between devices  493 us
    all_gather x1, waiting for transfers between devices, add_all(): parts = lax.all_gather(x, name)  283 us
    psum x1, waiting for transfers between devices, on_device(): lax.psum(glob_part.astype(jnp.bfloat16), 'ctx').astype(jnp.float32)  225 us
    all_gather x1, waiting for transfers between devices, on_device(): lax.all_gather(w_out, 'dp', axis=0, tiled=True)  55.8 us
  transfers between devices with their start and end apart: 8, of which 6 were waited for; matrix products, arithmetic and copies ran while one was open for 1% of the time, Pallas kernels for 0%

profile of v1, /device:TPU:1, one launch (start us, length us, event | category | flops | bytes accessed | tf_op | source)
XLA Modules:
  0.0 1127.8 jit_solution(4297355354902715088)
XLA Ops:
  8.0 0.9 constant_dynamic-update-slice_fusion.1
  8.9 0.9 constant_dynamic-update-slice_fusion
  10.6 1.1 fusion.18
  11.7 1.3 collective-permute-start.1
  13.0 5.0 collective-permute-start
  18.7 1.1 collective-permute-done.1
  19.8 1.5 collective-permute-done
  21.4 55.8 %all-gather.4.cloned.1.call-done = bf16[512,1024]{1,0:T(8,128)(2,1)} async-done(((bf16[32,1024]{1,0:T(8,128)(2,1)}), bf16[512,1024]{1,0:T(8,128)(2,1)}) %all-gather.4.cloned.1.call-update) | async-done | bytes 1048592 | tf_op jit(solution)/shard_map/all_gather | solution.py:76
  77.3 1.7 convolution_convert_fusion
  79.0 283.2 %all-gather.6.cloned.1.call-done = bf16[64,3,128,512]{3,2,1,0:T(8,128)(2,1)} async-done(((bf16[2,3,128,512]{3,2,1,0:T(8,128)(2,1)}), bf16[64,3,128,512]{3,2,1,0:T(8,128)(2,1)}) %all-gather.6.cloned.1.call-update) | async-done | bytes 25165840 | tf_op jit(solution)/shard_map/all_gather | solution.py:12
  362.2 13.0 %reduce_sum.94 = bf16[2,3,128,512]{3,2,1,0:T(8,128)(2,1)S(1)} reduce(bf16[32,2,3,128,512]{4,3,2,1,0:T(8,128)(2,1)} %bitcast.91, bf16[]{:T(256)} %constant.8.clone.1), dimensions={0}, to_apply=%region_2.0 | reduce | flops 12189696 | bytes 25952258 | tf_op jit(solution)/shard_map/reduce_sum | solution.py:13
  375.3 0.8 copy-done.3
  380.0 1.0 multiply_reduce_fusion.3
  388.3 2.1 pad_maximum_fusion.3
  390.5 1.6 pad_maximum_fusion.5
  392.1 2.0 collective-permute-start.3
  395.0 1.8 fusion.30
  396.8 0.9 copy-done.4
  397.8 1.3 collective-permute-start.2
  399.1 224.5 %all-reduce.5.cloned.1.call-done = bf16[2,3,128,512]{3,2,1,0:T(8,128)(2,1)} async-done(((bf16[2,3,128,512]{3,2,1,0:T(8,128)(2,1)}), bf16[2,3,128,512]{3,2,1,0:T(8,128)(2,1)}) %all-reduce.5.cloned.1.call-update) | async-done | bytes 786448 | tf_op jit(solution)/shard_map/psum | solution.py:152
  623.6 1.9 fusion.16
  625.6 1.1 fusion.21
  627.4 492.5 %all-reduce.7.cloned.1.call-done = f32[512,1024]{1,0:T(8,128)} async-done(((f32[512,1024]{1,0:T(8,128)}), f32[512,1024]{1,0:T(8,128)}) %all-reduce.7.cloned.1.call-update) | async-done | bytes 2097168
  1119.9 1.4 constant_dynamic-slice_fusion
  (91 shorter events, 15.0 us)
Async XLA Ops:
  7.2 70.1 %copy-start = (bf16[1,128,1024]{2,1,0:T(8,128)(2,1)S(1)}, bf16[1,128,1024]{2,1,0:T(8,128)(2,1)}, u32[]{:S(2)}) copy-start(bf16[1,128,1024]{2,1,0:T(8,128)(2,1)} %param.10) | copy-start | bytes 786436
  7.2 70.1 %all-gather.4.cloned.1.call-start = ((), (), s32[]{:S(2)}) async-start(), calls=%async_computation | async-start | bytes 1114112 | tf_op jit(solution)/shard_map/all_gather | solution.py:76
  7.9 354.3 %all-gather.6.cloned.1.call-start = ((), (), s32[]{:S(2)}) async-start(), calls=%async_computation.2 | async-start | bytes 25952256 | tf_op jit(solution)/shard_map/all_gather | solution.py:12
  8.9 9.2 copy-start.14
  8.9 9.5 copy-start.15
  11.7 611.9 %all-reduce.5.cloned.1.call-start = ((), (), s32[]{:S(2)}) async-start(), calls=%async_computation.1 | async-start | bytes 1572864 | tf_op jit(solution)/shard_map/psum | solution.py:152
  11.7 8.1 collective-permute-start.1
  13.0 8.3 collective-permute-start
  21.4 361.0 %copy-start.1 = (bf16[384,512]{1,0:T(8,128)(2,1)}, bf16[384,512]{1,0:T(8,128)(2,1)S(1)}, u32[]{:S(2)}) copy-start(bf16[384,512]{1,0:T(8,128)(2,1)S(1)} %get-tuple-element.31) | copy-start | bytes 1179652
  375.3 0.9 copy-start.3
  378.1 2.0 copy-start.7
  378.4 1.6 copy-start.9
  379.7 1.3 copy-start.11
  382.7 1.0 copy-start.2
  388.3 2.2 copy-start.6
  390.4 729.5 %all-reduce.7.cloned.1.call-start = ((), (), s32[]{:S(2)}) async-start(), calls=%async_computation.3 | async-start | bytes 4194304
  392.1 233.4 %collective-permute-start.3 = (bf16[2,128,512]{2,1,0:T(8,128)(2,1)}, bf16[2,128,512]{2,1,0:T(8,128)(2,1)}, u32[]{:S(2)}, u32[]{:S(2)}) collective-permute-start(bf16[2,128,512]{2,1,0:T(8,128)(2,1)} %pad_maximum_fusion.5), channel_id=1, source_target_pairs={{0,1},{1,2},{2,3},{3,4},{4,5},{5,6},{6,7},{7,8},{8,9},{9,10},{10,1... | collective-permute-start | bytes 786440 | tf_op jit(solution)/shard_map/ppermute | solution.py:32
  394.2 0.8 copy-start.8
  394.2 0.8 copy-start.10
  394.2 0.8 copy-start.12
  394.2 0.8 copy-start.13
  396.8 0.9 copy-start.4
  396.8 1.0 copy-start.5
  397.8 227.8 %collective-permute-start.2 = (bf16[2,128,512]{2,1,0:T(8,128)(2,1)S(1)}, bf16[2,128,512]{2,1,0:T(8,128)(2,1)S(1)}, u32[]{:S(2)}, u32[]{:S(2)}) collective-permute-start(bf16[2,128,512]{2,1,0:T(8,128)(2,1)S(1)} %pad_maximum_fusion.4), channel_id=1, source_target_pairs={{1,0},{2,1},{3,2},{4,3},{5,4},{6,5},{7,6},{8,7},{9,8},{10,9},{11,1... | collective-permute-start | bytes 786440 | tf_op jit(solution)/shard_map/ppermute | solution.py:32
Sparse Core Ops, SparseCore 0:
  11.4 65.8 all-gather.3
  79.4 282.8 all-gather.5
  390.5 233.0 all-reduce.4
  629.7 490.1 all-reduce.6
